TPU v7x, 512 devices: a whole 4x8x8 slice. The times are simulated.
512 devices in a mesh: ka: 64 (over z, y_lo, core), ga: 8 (over x, y_hi).
Axes of the slice: x: 4, y: 8 (y_hi: 2, y_lo: 4; y = y_hi * 4 + y_lo), z: 8, core: 2. Of those that a mesh axis runs over, the one named last changes fastest.
Arguments:
- wave_fields: bfloat16 [64, 16384, 2, 256], P('ka', 'ga'), may hold values from -6 to 6
- potential_change: bfloat16 [4, 2, 16384], P(None, None, 'ga'), may hold values from -0.046875 to 0.046875
- projectors: bfloat16 [4, 64, 16384], P(None, None, 'ga'), may hold values from -0.046875 to 0.046875
- mode_vectors: float32 [4, 3, 2, 8], replicated, may hold values from -6 to 6
- coupling_base: float32 [64, 64], replicated, may hold values from -4 to 4
- coupling_change: float32 [4, 2, 64, 64], replicated, may hold values from -4 to 4
- projector_atom: int32 [64], replicated, may hold values from 0 to 7, never falling along the last dimension, each value on 1 to 16 neighbouring positions
Outputs:
- matrix_elements: float32 [64, 256, 4, 2, 256], P('ka', 'ga')
Inputs may be any that keep to these rules, and one draw needn't show every extreme that they name: `projector_atom`: projectors of one atom stand together and atoms come in ascending order; every atom has 1 to 16 projectors, and some atom has exactly 16.
All inputs are finite; a program needn't handle non-finite values.
Results may differ from a plain program's by a relative error of at most 0.001.
Values may be sent and summed in bfloat16 or wider, within the bound.
A program may use at most 64 MiB of HBM per device.

v0:
```python
import jax
import jax.numpy as jnp
from jax import lax
from jax.sharding import PartitionSpec as P


def from_behind(value, axis, steps):
    count = lax.axis_size(axis)
    pairs = [(source, (source + steps) % count) for source in range(count)]
    return lax.ppermute(value, axis, pairs)


def weight_waves(own_bands, potential_change):
    wave_real = own_bands[:, 0].astype(jnp.float32)
    wave_imag = own_bands[:, 1].astype(jnp.float32)
    pot_real = potential_change[:, 0].astype(jnp.float32).T
    pot_imag = potential_change[:, 1].astype(jnp.float32).T
    out_real = (
        pot_real[:, :, None] * wave_real[:, None, :] - pot_imag[:, :, None] * wave_imag[:, None, :]
    )
    out_imag = (
        pot_real[:, :, None] * wave_imag[:, None, :] + pot_imag[:, :, None] * wave_real[:, None, :]
    )
    return jnp.stack([out_real, out_imag], axis=1).astype(jnp.bfloat16)


def paired_rows(partner_rows):
    real_part = partner_rows[:, 0]
    imag_part = partner_rows[:, 1]
    return jnp.stack(
        [jnp.stack([real_part, -imag_part], axis=1), jnp.stack([imag_part, real_part], axis=1)],
        axis=1,
    )


def nonlocal_terms(
    own_proj, partner_proj, mode_vectors, coupling_base, coupling_change, projector_atom
):
    highest = lax.Precision.HIGHEST
    atoms = mode_vectors.shape[-1]
    onehot_atoms = (projector_atom[:, None] == jnp.arange(atoms, dtype=jnp.int32)[None, :]).astype(
        jnp.float32
    )
    same_atom = (projector_atom[:, None] == projector_atom[None, :]).astype(jnp.float32)
    base_masked = 0.5 * (coupling_base + coupling_base.T) * same_atom
    change_masked = coupling_change * same_atom
    mode_proj = jnp.einsum("vcxa,ia->vcxi", mode_vectors, onehot_atoms, precision=highest)
    vec_real = mode_proj[:, :, 0]
    vec_imag = mode_proj[:, :, 1]
    own_real = own_proj[0, :, 0]
    own_imag = own_proj[0, :, 1]
    grad_real = own_proj[1:, :, 0]
    grad_imag = own_proj[1:, :, 1]
    part_real = partner_proj[0, :, 0]
    part_imag = partner_proj[0, :, 1]
    pgrad_real = partner_proj[1:, :, 0]
    pgrad_imag = partner_proj[1:, :, 1]

    def contract(left_side, right_side):
        return jnp.einsum("vci,cin->vin", left_side, right_side, precision=highest)

    shift_real = -(contract(vec_real, grad_real) - contract(vec_imag, grad_imag))
    shift_imag = -(contract(vec_real, grad_imag) + contract(vec_imag, grad_real))
    bra_real = -(contract(vec_real, pgrad_real) + contract(vec_imag, pgrad_imag))
    bra_imag = -(contract(vec_imag, pgrad_real) - contract(vec_real, pgrad_imag))
    base_real = jnp.einsum("ij,jn->in", base_masked, own_real, precision=highest)
    base_imag = jnp.einsum("ij,jn->in", base_masked, own_imag, precision=highest)
    first_real = jnp.einsum("vim,in->vmn", bra_real, base_real, precision=highest) - jnp.einsum(
        "vim,in->vmn", bra_imag, base_imag, precision=highest
    )
    first_imag = jnp.einsum("vim,in->vmn", bra_real, base_imag, precision=highest) + jnp.einsum(
        "vim,in->vmn", bra_imag, base_real, precision=highest
    )
    change_real = change_masked[:, 0]
    change_imag = change_masked[:, 1]
    inner_real = jnp.einsum("ij,vjn->vin", base_masked, shift_real, precision=highest)
    inner_imag = jnp.einsum("ij,vjn->vin", base_masked, shift_imag, precision=highest)
    inner_real = (
        inner_real
        + jnp.einsum("vij,jn->vin", change_real, own_real, precision=highest)
        - jnp.einsum("vij,jn->vin", change_imag, own_imag, precision=highest)
    )
    inner_imag = (
        inner_imag
        + jnp.einsum("vij,jn->vin", change_real, own_imag, precision=highest)
        + jnp.einsum("vij,jn->vin", change_imag, own_real, precision=highest)
    )
    tail_real = jnp.einsum("im,vin->vmn", part_real, inner_real, precision=highest) + jnp.einsum(
        "im,vin->vmn", part_imag, inner_imag, precision=highest
    )
    tail_imag = jnp.einsum("im,vin->vmn", part_real, inner_imag, precision=highest) - jnp.einsum(
        "im,vin->vmn", part_imag, inner_real, precision=highest
    )
    total = jnp.stack([first_real + tail_real, first_imag + tail_imag], axis=2)
    return jnp.transpose(total, (1, 0, 2, 3))


def body(
    wave_fields,
    potential_change,
    projectors,
    mode_vectors,
    coupling_base,
    coupling_change,
    projector_atom,
):
    own_bands = wave_fields[0]
    grid_points = own_bands.shape[0]
    bands = own_bands.shape[2]
    proj_count = projectors.shape[1]
    pool_count = lax.axis_size("ka")
    slab_count = lax.axis_size("ga")
    rows_here = bands // slab_count
    first_row = lax.axis_index("ga") * rows_here
    partner = from_behind(own_bands, "ka", -(pool_count // 4))
    stacked = projectors.reshape(4 * proj_count, grid_points)
    own_part = jnp.dot(
        stacked, own_bands.reshape(grid_points, 2 * bands), preferred_element_type=jnp.float32
    ).reshape(4, proj_count, 2, bands)
    weighted = weight_waves(own_bands, potential_change)
    own_proj = lax.psum(own_part, "ga")
    own_slice = lax.dynamic_slice_in_dim(own_proj, first_row, rows_here, 3)
    partner_rows = from_behind(own_slice, "ka", -(pool_count // 4))
    paired = paired_rows(partner)
    summed = lax.dot_general(
        paired, weighted, (((0, 1), (0, 1)), ((), ())), preferred_element_type=jnp.float32
    )
    local_sum = lax.psum_scatter(
        jnp.transpose(summed, (1, 2, 0, 3)).astype(jnp.bfloat16),
        "ga",
        scatter_dimension=0,
        tiled=True,
    ).astype(jnp.float32)
    nonlocal_part = nonlocal_terms(
        own_proj, partner_rows, mode_vectors, coupling_base, coupling_change, projector_atom
    )
    return (local_sum + nonlocal_part)[None]


def solution(mesh):
    placed = (
        P("ka", "ga", None, None),
        P(None, None, "ga"),
        P(None, None, "ga"),
        P(),
        P(),
        P(),
        P(),
    )
    return jax.shard_map(
        body, mesh=mesh, in_specs=placed, out_specs=P("ka", "ga", None, None, None), check_vma=False
    )
```

profile of v0, /device:TPU:6, one launch (start us, length us, event | category | flops | bytes accessed | tf_op | source)
XLA Modules:
  0.0 261.7 jit_solution(2366366998085604584)
XLA Ops:
  6.5 2.1 copy.80
  8.7 2.5 copy.37
  11.1 3.1 %fusion.18 = f32[4,64,2,256]{3,1,2,0:T(8,128)} fusion(bf16[2,256,2048,1]{2,1,0,3:T(8,128)(2,1)} %bitcast.200, bf16[4,64,2048]{2,1,0:T(8,128)(2,1)S(1)} %copy-done), kind=kOutput, calls=%fused_computation.42 | convolution fusion | flops 536870912 | bytes 3670016 | tf_op jit(solution)/shard_map/dot_general | solution.py:117
  14.3 4.7 %copy.33 = bf16[1,2048,2,256]{1,3,2,0:T(8,128)(2,1)S(1)} copy(bf16[1,2048,2,256]{3,2,1,0:T(2,128)(2,1)} %param.7) | data formatting | bytes 4194304 | tf_op args[0]
  19.1 11.1 %collective-permute-start = (bf16[2048,2,256]{0,2,1:T(8,128)(2,1)S(1)}, bf16[2048,2,256]{0,2,1:T(8,128)(2,1)}, u32[]{:S(2)}, u32[]{:S(2)}) collective-permute-start(bf16[2048,2,256]{0,2,1:T(8,128)(2,1)S(1)} %bitcast.196), channel_id=1, source_target_pairs={{0,384},{8,392},{16,400},{24,408},{32,416},{40,424},{48,432},{56,4... | collective-permute-start | bytes 6291464 | tf_op jit(solution)/shard_map/ppermute | solution.py:10
  30.2 2.5 fusion.17
  33.4 0.9 slice_convert_fusion.1
  34.3 2.9 %copy.35 = f32[2048,256]{1,0:T(8,128)} copy(f32[2048,256]{0,1:T(8,128)} %get-tuple-element.10) | data formatting | bytes 4194304 | tf_op jit(solution)/shard_map/mul | solution.py:19
  37.2 2.9 %copy.36 = f32[2048,256]{1,0:T(8,128)} copy(f32[2048,256]{0,1:T(8,128)} %get-tuple-element.11) | data formatting | bytes 4194304 | tf_op jit(solution)/shard_map/mul | solution.py:19
  40.1 1.7 copy_multiply_fusion
  41.8 7.5 %subtract_convert_fusion = (bf16[2048,1,4,256]{3,0,1,2:T(8,128)(2,1)}, bf16[2048,1,4,256]{3,0,1,2:T(8,128)(2,1)}) fusion(f32[2048,256]{1,0:T(8,128)} %copy.36, f32[2048,4]{0,1:T(4,128)S(1)} %get-tuple-element.22, f32[2048,256]{1,0:T(8,128)} %copy.35, f32[2048,4]{0,1:T(4,128)S(1)} %get-tuple-element.23), kind=kLoop, calls=%fused_computation.5 | loop fusion | flops 16777216 | bytes 12648448 | tf_op jit(solution)/shard_map/convert.6
  49.3 84.8 %all-reduce.2.cloned.1.call-done = f32[4,64,2,256]{3,1,2,0:T(8,128)} async-done(((f32[4,64,2,256]{3,1,2,0:T(8,128)}), f32[4,64,2,256]{3,1,2,0:T(8,128)}) %all-reduce.2.cloned.1.call-update) | async-done | bytes 524304 | tf_op jit(solution)/shard_map/psum | solution.py:121
  134.1 1.1 slice_bitcast_fusion.3
  135.2 0.8 fusion.20
  136.0 0.8 fusion.22
  136.8 0.8 fusion.24
  137.6 0.8 fusion.26
  138.3 1.1 constant_dynamic-slice_fusion
  139.4 6.8 %collective-permute-start.1 = (f32[4,64,2,32]{3,1,2,0:T(8,128)S(1)}, f32[4,64,2,32]{3,1,2,0:T(8,128)S(1)}, u32[]{:S(2)}, u32[]{:S(2)}) collective-permute-start(f32[4,64,2,32]{3,1,2,0:T(8,128)S(1)} %constant_dynamic-slice_fusion), channel_id=1, source_target_pairs={{0,384},{8,392},{16,400},{24,408},{32,416},{40,424},{48,432},{56,4... | collective-permute-start | bytes 196616 | tf_op jit(solution)/shard_map/ppermute | solution.py:10
  146.3 0.5 convolution_bitcast_fusion
  146.7 0.8 convolution_bitcast_fusion.3
  147.6 0.3 convolution_add_fusion.1
  147.9 1.1 convolution_add_fusion
  149.0 0.5 convolution_bitcast_fusion.1
  149.4 0.3 convolution_add_fusion.2
  149.8 1.1 convolution_subtract_fusion
  150.9 0.8 convolution_bitcast_fusion.2
  151.7 1.3 collective-permute-done.1
  153.0 0.7 copy-done.12
  153.7 0.7 fusion.40
  154.4 1.3 fusion.15
  155.8 1.6 copy.44
  157.4 1.9 slice_negate_fusion
  159.3 0.4 maximum_bitcast_fusion.4
  159.7 0.5 copy-done.2
  160.2 1.5 copy-done.1
  161.7 5.5 %fusion.5 = bf16[256,4,2,256]{3,0,1,2:T(8,128)(2,1)} fusion(bf16[2048,1,4,256]{3,0,1,2:T(8,128)(2,1)S(1)} %copy-done.2, bf16[2048,1,4,256]{3,0,1,2:T(8,128)(2,1)S(1)} %copy-done.1, bf16[2048,1,2,256]{0,3,1,2:T(8,128)(2,1)S(1)} %get-tuple-element.13, bf16[2048,1,2,256]{0,3,1,2:T(8,128)(2,1)S(1)} %get-tuple-element.12), kind=kOutput, calls=%fused_computation.12 | convolution fusion | flops 4320657408 | bytes 13631488 | tf_op jit(solution)/shard_map/dot_general | solution.py:125
  167.3 0.7 fusion.38
  168.0 0.7 fusion.13
  168.8 0.2 fusion.66
  169.3 0.3 fusion.60
  169.7 0.3 fusion.11
  170.2 0.2 convolution_add_fusion.3
  170.5 0.3 fusion.59
  170.8 0.3 fusion.8
  171.1 81.9 %reduce-scatter.2.cloned.1.call-done = bf16[32,4,2,256]{3,0,1,2:T(8,128)(2,1)} async-done(((bf16[256,4,2,256]{3,0,1,2:T(8,128)(2,1)}), bf16[32,4,2,256]{3,0,1,2:T(8,128)(2,1)}) %reduce-scatter.2.cloned.1.call-update) | async-done | bytes 131088 | tf_op jit(solution)/shard_map/reduce_scatter | solution.py:128
  253.0 0.9 fusion.29
  254.0 0.9 copy.57
  (48 shorter events, 1.4 us)
Async XLA Ops:
  6.5 4.6 %copy-start = (bf16[4,64,2048]{2,1,0:T(8,128)(2,1)S(1)}, bf16[4,64,2048]{2,1,0:T(8,128)(2,1)}, u32[]{:S(2)}) copy-start(bf16[4,64,2048]{2,1,0:T(8,128)(2,1)} %param.9) | copy-start | bytes 3145732
  6.5 127.6 %all-reduce.2.cloned.1.call-start = ((), (), s32[]{:S(2)}) async-start(), calls=%async_computation.2 | async-start | bytes 1048576 | tf_op jit(solution)/shard_map/psum | solution.py:121
  14.3 238.7 %reduce-scatter.2.cloned.1.call-start = ((), (), s32[]{:S(2)}) async-start(), calls=%async_computation.1 | async-start | bytes 1179648 | tf_op jit(solution)/shard_map/reduce_scatter | solution.py:128
  19.1 13.6 %copy-start.15 = (s32[64]{0:T(128)S(1)}, s32[64]{0:T(128)}, u32[]{:S(2)}) copy-start(s32[64]{0:T(128)} %param.13) | copy-start | bytes 772
  19.1 13.7 %copy-start.16 = (f32[4,3,2,8]{3,2,1,0:T(2,128)S(1)}, f32[4,3,2,8]{3,2,1,0:T(2,128)}, u32[]{:S(2)}) copy-start(f32[4,3,2,8]{3,2,1,0:T(2,128)} %param.10) | copy-start | bytes 2308
  19.1 14.1 %copy-start.14 = (f32[64,64]{1,0:T(8,128)S(1)}, f32[64,64]{1,0:T(8,128)}, u32[]{:S(2)}) copy-start(f32[64,64]{1,0:T(8,128)} %param.11) | copy-start | bytes 49156
  19.1 138.3 %collective-permute-start = (bf16[2048,2,256]{0,2,1:T(8,128)(2,1)S(1)}, bf16[2048,2,256]{0,2,1:T(8,128)(2,1)}, u32[]{:S(2)}, u32[]{:S(2)}) collective-permute-start(bf16[2048,2,256]{0,2,1:T(8,128)(2,1)S(1)} %bitcast.196), channel_id=1, source_target_pairs={{0,384},{8,392},{16,400},{24,408},{32,416},{40,424},{48,432},{56,4... | collective-permute-start | bytes 6291464 | tf_op jit(solution)/shard_map/ppermute | solution.py:10
  134.1 12.6 %copy-start.6 = (f32[4,64,2,256]{3,1,2,0:T(8,128)S(1)}, f32[4,64,2,256]{3,1,2,0:T(8,128)}, u32[]{:S(2)}) copy-start(f32[4,64,2,256]{3,1,2,0:T(8,128)} %all-reduce.2.cloned.1.call-done) | copy-start | bytes 1572868
  134.1 13.4 %copy-start.5 = (f32[4,2,64,64]{3,2,0,1:T(8,128)S(1)}, f32[4,2,64,64]{3,2,0,1:T(8,128)}, u32[]{:S(2)}) copy-start(f32[4,2,64,64]{3,2,0,1:T(8,128)} %copy_multiply_fusion) | copy-start | bytes 393220
  139.4 13.6 %collective-permute-start.1 = (f32[4,64,2,32]{3,1,2,0:T(8,128)S(1)}, f32[4,64,2,32]{3,1,2,0:T(8,128)S(1)}, u32[]{:S(2)}, u32[]{:S(2)}) collective-permute-start(f32[4,64,2,32]{3,1,2,0:T(8,128)S(1)} %constant_dynamic-slice_fusion), channel_id=1, source_target_pairs={{0,384},{8,392},{16,400},{24,408},{32,416},{40,424},{48,432},{56,4... | collective-permute-start | bytes 196616 | tf_op jit(solution)/shard_map/ppermute | solution.py:10
  153.0 0.7 copy-start.12
  153.7 0.7 copy-start.7
  157.4 2.8 %copy-start.2 = (bf16[2048,1,4,256]{3,0,1,2:T(8,128)(2,1)S(1)}, bf16[2048,1,4,256]{3,0,1,2:T(8,128)(2,1)}, u32[]{:S(2)}) copy-start(bf16[2048,1,4,256]{3,0,1,2:T(8,128)(2,1)} %get-tuple-element.6) | copy-start | bytes 12582916
  159.3 2.4 copy-start.1
  161.7 6.3 %copy-start.8 = (f32[3,64,32]{2,1,0:T(8,128)S(1)}, f32[3,64,32]{2,1,0:T(8,128)}, u32[]{:S(2)}) copy-start(f32[3,64,32]{2,1,0:T(8,128)} %copy-done.7) | copy-start | bytes 73732
  161.7 7.1 %copy-start.9 = (f32[4,64,32]{1,2,0:T(8,128)S(1)}, f32[4,64,32]{1,2,0:T(8,128)}, u32[]{:S(2)}) copy-start(f32[4,64,32]{1,2,0:T(8,128)} %copy.44) | copy-start | bytes 98308
  161.7 7.1 %copy-start.10 = (f32[64,256,1]{1,0,2:T(8,128)S(1)}, f32[64,256,1]{1,0,2:T(8,128)}, u32[]{:S(2)}) copy-start(f32[64,256,1]{1,0,2:T(8,128)} %convolution_bitcast_fusion.3) | copy-start | bytes 196612
  161.7 7.3 %copy-start.11 = (f32[64,256,1]{1,0,2:T(8,128)S(1)}, f32[64,256,1]{1,0,2:T(8,128)}, u32[]{:S(2)}) copy-start(f32[64,256,1]{1,0,2:T(8,128)} %convolution_bitcast_fusion.2) | copy-start | bytes 196612
  161.7 7.6 %copy-start.3 = (f32[4,64,256]{2,1,0:T(8,128)S(1)}, f32[4,64,256]{2,1,0:T(8,128)}, u32[]{:S(2)}) copy-start(f32[4,64,256]{2,1,0:T(8,128)} %convolution_add_fusion) | copy-start | bytes 786436
  161.7 7.6 %copy-start.13 = (f32[4,64,2,32]{3,1,2,0:T(8,128)S(1)}, f32[4,64,2,32]{3,1,2,0:T(8,128)}, u32[]{:S(2)}) copy-start(f32[4,64,2,32]{3,1,2,0:T(8,128)} %copy-done.12) | copy-start | bytes 196612
  161.7 7.9 %copy-start.4 = (f32[4,64,256]{2,1,0:T(8,128)S(1)}, f32[4,64,256]{2,1,0:T(8,128)}, u32[]{:S(2)}) copy-start(f32[4,64,256]{2,1,0:T(8,128)} %convolution_subtract_fusion) | copy-start | bytes 786436
Sparse Core Ops, SparseCore 0:
  14.4 119.6 all-reduce.1
  167.4 85.5 reduce-scatter.1
where the time goes:
time: 263 us; the launch traced here: 262 us
  waiting for transfers between devices  168 us (64%)
  local copies, waits for them, and re-layouts  23.1 us (9%)
  matrix products  22.9 us (9%)
  starting transfers between devices  17.9 us (7%)
  other arithmetic  16 us (6%)
  between operations  13.8 us (5%)
    psum x1, waiting for transfers between devices, body(): own_proj = lax.psum(own_part, 'ga')  84.8 us
    reduce_scatter x1, waiting for transfers between devices, body(): lax.psum_scatter(jnp.transpose(summed, (1, 2, 0, 3)).astype(jnp.bfloat16)...  81.9 us
    ppermute x2, starting transfers between devices, from_behind(): return lax.ppermute(value, axis, pairs)  17.9 us
    unnamed x37, local copies, waits for them, and re-layouts  9.72 us
    another operation x1, other arithmetic  7.52 us
    dot_general x8, matrix products, contract(): return jnp.einsum('vci,cin->vin', left_side, right_side, precision=highest)  6.47 us
    dot_general x1, matrix products, body(): lax.dot_general(paired, weighted, (((0, 1), (0, 1)), ((), ())), preferred...  5.52 us
  transfers between devices with their start and end apart: 4, of which 3 were waited for; matrix products, arithmetic and copies ran while one was open for 16% of the time, Pallas kernels for 0%

commit v1 on v0

v1 whole, which is shorter than its diff:
```python
import functools

import jax
import jax.numpy as jnp
from jax import lax
from jax.experimental import pallas as pl
from jax.experimental.pallas import tpu as pltpu
from jax.sharding import PartitionSpec as P

MESH = pl.DeviceIdType.MESH
F32 = jnp.float32
BF16 = jnp.bfloat16
HIGHEST = lax.Precision.HIGHEST
MODES = 4
GROUPS = 4
AHEAD = 3


def dot_nn(left, right, precision=None):
    return jnp.dot(left, right, preferred_element_type=F32, precision=precision)


def dot_nt(left, right, precision=None):
    return lax.dot_general(
        left, right, (((1,), (1,)), ((), ())), preferred_element_type=F32, precision=precision
    )


def nonlocal_rows(rows_ref, all_proj, vec_rows, base_ref, change_ref, same, mixed, result):
    count = same.shape[0]
    rows = rows_ref.shape[1]
    base = 0.5 * (base_ref[...] + base_ref[...].T) * same
    conj_re = rows_ref[0]
    conj_im = -rows_ref[1]

    def group(value, j):
        return value[:, j * count : (j + 1) * count]

    def vec(mode, c):
        at = (mode * 3 + c) * 2
        return vec_rows[at : at + 1, :], vec_rows[at + 1 : at + 2, :]

    bra = []
    for mode in range(MODES):
        total_re = jnp.zeros((rows, count), F32)
        total_im = jnp.zeros((rows, count), F32)
        for c in range(3):
            v_re, v_im = vec(mode, c)
            g_re, g_im = group(conj_re, c + 1), group(conj_im, c + 1)
            total_re = total_re - (v_re * g_re - v_im * g_im)
            total_im = total_im - (v_re * g_im + v_im * g_re)
        bra += [total_re, total_im]
    bra_base = dot_nn(jnp.concatenate(bra, axis=0), base, HIGHEST)
    value = jnp.concatenate([group(conj_re, 0), group(conj_im, 0)], axis=0)
    value_base = dot_nn(value, base, HIGHEST)
    t_re, t_im = value_base[:rows], value_base[rows:]
    for mode in range(MODES):
        with_re = dot_nn(value, change_ref[mode, 0] * same, HIGHEST)
        with_im = dot_nn(value, change_ref[mode, 1] * same, HIGHEST)
        at = mode * 2 * rows
        mixed[at : at + rows, 0:count] = bra_base[at : at + rows] + with_re[:rows] - with_im[rows:]
        mixed[at + rows : at + 2 * rows, 0:count] = (
            bra_base[at + rows : at + 2 * rows] + with_im[:rows] + with_re[rows:]
        )
        for c in range(3):
            v_re, v_im = vec(mode, c)
            lanes = slice((c + 1) * count, (c + 2) * count)
            mixed[at : at + rows, lanes] = -(t_re * v_re - t_im * v_im)
            mixed[at + rows : at + 2 * rows, lanes] = -(t_re * v_im + t_im * v_re)
    by_re = dot_nt(mixed[...], all_proj[0], HIGHEST)
    by_im = dot_nt(mixed[...], all_proj[1], HIGHEST)
    bands = by_re.shape[1]
    for mode in range(MODES):
        at = mode * 2 * rows
        re, im = slice(at, at + rows), slice(at + rows, at + 2 * rows)
        lane = mode * 2 * bands
        result[:, lane : lane + bands] = by_re[re] - by_im[im]
        result[:, lane + bands : lane + 2 * bands] = by_im[re] + by_re[im]


def kernel(
    sizes,
    turned,
    flat,
    pot_rows,
    pot_cols,
    projectors,
    vec_in,
    base_ref,
    change_ref,
    atom_row,
    atom_col,
    out_ref,
    landing,
    weighted,
    weighted_t,
    proj_part,
    proj_land,
    proj_own,
    all_proj,
    rows_land,
    mixed,
    nonlocal_sum,
    sum_send,
    sum_land,
    piece_send,
    piece_land,
    last_rows,
    back_send,
    back_land,
    stream_send,
    stream_recv,
    part_send,
    part_recv,
    all_send,
    all_recv,
    rows_send_sem,
    rows_recv_sem,
    sum_send_sem,
    sum_recv_sem,
    back_send_sem,
    back_recv_sem,
):
    pools, slabs, points, bands = sizes
    rows = bands // slabs
    step = pools // 4
    ka = lax.axis_index("ka")
    ga = lax.axis_index("ga")
    core = lax.rem(ka, 2)
    ahead_k = lax.rem(ka + step, pools)
    behind_k = lax.rem(ka + pools - step, pools)

    barrier = pltpu.get_barrier_semaphore()
    for d in range(1, slabs):
        pl.semaphore_signal(
            barrier, inc=1, device_id=(ka, lax.rem(ga + d, slabs)), device_id_type=MESH
        )
    for other in (ahead_k, behind_k):
        pl.semaphore_signal(barrier, inc=1, device_id=(other, ga), device_id_type=MESH)
    pl.semaphore_wait(barrier, slabs + 1)

    target_k = jnp.where(core == 0, ahead_k, behind_k)
    first_chunk = jnp.where(core == 0, 0, ga + 1)

    def stream(s):
        chunk = lax.rem(first_chunk + s, slabs)
        return pltpu.make_async_remote_copy(
            src_ref=turned.at[chunk],
            dst_ref=landing.at[s],
            send_sem=stream_send.at[s],
            recv_sem=stream_recv.at[s],
            device_id=(target_k, ga),
            device_id_type=MESH,
        )

    for s in range(AHEAD):
        stream(s).start()

    for j in range(slabs):
        proj_part[j] = dot_nt(turned[j], projectors[...])

    def part_copy(d):
        peer = lax.rem(ga + d, slabs)
        return pltpu.make_async_remote_copy(
            src_ref=proj_part.at[peer],
            dst_ref=proj_land.at[d],
            send_sem=part_send.at[d],
            recv_sem=part_recv.at[d],
            device_id=(ka, peer),
            device_id_type=MESH,
        )

    for d in range(1, slabs):
        part_copy(d).start()

    @pl.when(core == 1)
    def _():
        block = 128

        def weigh(i, carry):
            at = pl.ds(pl.multiple_of(i * block, block), block)
            re = flat[at, 0:bands].astype(F32)
            im = flat[at, bands : 2 * bands].astype(F32)
            cols = pot_cols[at, :]
            for mode in range(MODES):
                p_re = cols[:, 2 * mode : 2 * mode + 1]
                p_im = cols[:, 2 * mode + 1 : 2 * mode + 2]
                lane = mode * 2 * bands
                weighted[at, lane : lane + bands] = (p_re * re - p_im * im).astype(BF16)
                weighted[at, lane + bands : lane + 2 * bands] = (p_re * im + p_im * re).astype(BF16)
            return carry

        lax.fori_loop(0, points // block, weigh, 0)

    total = proj_part[ga]
    for d in range(1, slabs):
        part_copy(d).wait_recv()
    for d in range(1, slabs):
        total = total + proj_land[d]
    proj_own[0] = total[:rows]
    proj_own[1] = total[rows:]
    own_rows = pl.ds(pl.multiple_of(ga * rows, rows), rows)
    all_proj[0, own_rows, :] = total[:rows]
    all_proj[1, own_rows, :] = total[rows:]

    def all_copy(d):
        return pltpu.make_async_remote_copy(
            src_ref=proj_own,
            dst_ref=all_proj.at[:, own_rows, :],
            send_sem=all_send.at[d],
            recv_sem=all_recv.at[d],
            device_id=(ka, lax.rem(ga + d, slabs)),
            device_id_type=MESH,
        )

    rows_copy = pltpu.make_async_remote_copy(
        src_ref=proj_own,
        dst_ref=rows_land,
        send_sem=rows_send_sem,
        recv_sem=rows_recv_sem,
        device_id=(behind_k, ga),
        device_id_type=MESH,
    )
    rows_copy.start()
    for d in range(1, slabs):
        all_copy(d).start()

    def all_arrival(d):
        peer = lax.rem(ga + slabs - d, slabs)
        theirs = pl.ds(pl.multiple_of(peer * rows, rows), rows)
        return pltpu.make_async_remote_copy(
            src_ref=proj_own,
            dst_ref=all_proj.at[:, theirs, :],
            send_sem=all_send.at[d],
            recv_sem=all_recv.at[d],
            device_id=(ka, peer),
            device_id_type=MESH,
        )

    def nonlocal_part():
        for d in range(1, slabs):
            all_arrival(d).wait_recv()
        rows_copy.wait_recv()
        atoms = vec_in.shape[1]
        onehot = (
            lax.broadcasted_iota(jnp.int32, (atoms, atom_row.shape[1]), 0) == atom_row[...]
        ).astype(F32)
        vec_rows = dot_nn(vec_in[...], onehot, HIGHEST)
        same = (atom_col[...] == atom_row[...]).astype(F32)
        nonlocal_rows(
            rows_land, all_proj, vec_rows, base_ref, change_ref, same, mixed, nonlocal_sum
        )

    def next_chunk(s):
        stream(s).wait_recv()
        stream(s).wait_send()

        @pl.when(s + AHEAD < slabs)
        def _():
            stream(s + AHEAD).start()

    @pl.when(core == 1)
    def _():
        def rows_copy_to(s):
            return pltpu.make_async_remote_copy(
                src_ref=sum_send.at[s],
                dst_ref=sum_land.at[s],
                send_sem=sum_send_sem.at[s, 0],
                recv_sem=sum_recv_sem.at[s, 0],
                device_id=(ka, lax.rem(ga + 1 + s, slabs)),
                device_id_type=MESH,
            )

        def chunk_sum(s, put):
            for mode in range(MODES):
                lane = mode * 2 * bands
                both = dot_nn(landing[s], weighted[:, lane : lane + 2 * bands])
                put(lane, both[:rows, :bands] + both[rows:, bands:])
                put(lane + bands, both[:rows, bands:] - both[rows:, :bands])

        def one(s, carry):
            next_chunk(s)

            def put(lane, value):
                sum_send[s, :, lane : lane + bands] = value.astype(BF16)

            chunk_sum(s, put)
            rows_copy_to(s).start()
            return carry

        lax.fori_loop(0, 3, one, 0)
        nonlocal_part()
        lax.fori_loop(3, slabs - 1, one, 0)
        next_chunk(slabs - 1)

        def put_last(lane, value):
            last_rows[:, lane : lane + bands] = value + nonlocal_sum[:, lane : lane + bands]

        chunk_sum(slabs - 1, put_last)
        for s in range(slabs - 1):
            rows_copy_to(s).wait_recv()
        for lane in range(0, 2 * MODES * bands, bands):
            value = last_rows[:, lane : lane + bands]
            for s in range(slabs - 1):
                value = value + sum_land[s, :, lane : lane + bands].astype(F32)
            out_ref[:, lane : lane + bands] = value
        for s in range(slabs - 1):
            rows_copy_to(s).wait_send()

    @pl.when(core == 0)
    def _():
        def piece_copy(s, d):
            peer = lax.rem(ga + d, slabs)
            return pltpu.make_async_remote_copy(
                src_ref=piece_send.at[s, pl.ds(pl.multiple_of(peer * rows, rows), rows)],
                dst_ref=piece_land.at[s, pl.ds(d * rows, rows)],
                send_sem=sum_send_sem.at[s, d],
                recv_sem=sum_recv_sem.at[s, d],
                device_id=(ka, peer),
                device_id_type=MESH,
            )

        def back_copy(s):
            return pltpu.make_async_remote_copy(
                src_ref=back_send.at[s],
                dst_ref=back_land.at[s],
                send_sem=back_send_sem.at[s],
                recv_sem=back_recv_sem.at[s],
                device_id=(behind_k, ga),
                device_id_type=MESH,
            )

        def chunk_sum(s):
            block = 512
            for at in range(0, points, block):
                re = landing[s, 0:rows, at : at + block].astype(F32)
                im = landing[s, rows : 2 * rows, at : at + block].astype(F32)
                for mode in range(MODES):
                    p_re = pot_rows[2 * mode : 2 * mode + 1, at : at + block]
                    p_im = pot_rows[2 * mode + 1 : 2 * mode + 2, at : at + block]
                    top = mode * rows
                    weighted_t[top : top + rows, at : at + block] = (p_re * re - p_im * im).astype(
                        BF16
                    )
                    top = (MODES + mode) * rows
                    weighted_t[top : top + rows, at : at + block] = (p_re * im + p_im * re).astype(
                        BF16
                    )
            both = dot_nn(weighted_t[...], flat[...])
            half = MODES * rows
            real = both[:half, :bands] + both[half:, bands:]
            imag = both[half:, :bands] - both[:half, bands:]
            piece_send[s, :, 0:half] = real.T.astype(BF16)
            piece_send[s, :, half : 2 * half] = imag.T.astype(BF16)
            for d in range(1, slabs):
                piece_copy(s, d).start()

        def reduce(s):
            value = piece_send[s, own_rows].astype(F32)
            for d in range(1, slabs):
                piece_copy(s, d).wait_recv()
            for d in range(1, slabs):
                value = value + piece_land[s, d * rows : (d + 1) * rows].astype(F32)
            back_send[s] = value.astype(BF16)
            back_copy(s).start()

        def one(s, carry):
            next_chunk(s)
            chunk_sum(s)

            @pl.when(s > 0)
            def _():
                reduce(s - 1)

            return carry

        lax.fori_loop(0, 3, one, 0)
        nonlocal_part()
        lax.fori_loop(3, slabs, one, 0)
        reduce(slabs - 1)
        for s in range(slabs):
            back_copy(s).wait_recv()
        width = 128
        per = width // rows
        at_lane = lax.broadcasted_iota(jnp.int32, (rows, width), 1)
        for mode in range(MODES):
            for part in range(2):
                for q in range(bands // width):
                    value = jnp.zeros((rows, width), F32)
                    for t in range(per):
                        piece = back_land[q * per + t, :, part * width : (part + 1) * width].astype(
                            F32
                        )
                        shift = (t - mode) * rows % width
                        if shift:
                            piece = pltpu.roll(piece, shift, 1)
                        inside = (at_lane >= t * rows) & (at_lane < (t + 1) * rows)
                        value = jnp.where(inside, piece, value)
                    lane = (mode * 2 + part) * bands + q * width
                    out_ref[:, lane : lane + width] = value + nonlocal_sum[:, lane : lane + width]
        for s in range(slabs):
            back_copy(s).wait_send()
            for d in range(1, slabs):
                piece_copy(s, d).wait_send()

    for d in range(1, slabs):
        part_copy(d).wait_send()
        all_copy(d).wait_send()
    rows_copy.wait_send()


def body(
    wave_fields,
    potential_change,
    projectors,
    mode_vectors,
    coupling_base,
    coupling_change,
    projector_atom,
):
    own = wave_fields[0]
    points, _, bands = own.shape
    pools, slabs = lax.axis_size("ka"), lax.axis_size("ga")
    count = projectors.shape[1]
    atoms = mode_vectors.shape[-1]
    rows = bands // slabs
    turned = jnp.transpose(own.reshape(points, 2, slabs, rows), (2, 1, 3, 0))
    turned = turned.reshape(slabs, 2 * rows, points)
    flat = own.reshape(points, 2 * bands)
    pot_rows = potential_change.reshape(2 * MODES, points).astype(F32)
    wide = 2 * MODES * bands
    vmem = pl.BlockSpec(memory_space=pltpu.VMEM)
    dma = pltpu.SemaphoreType.DMA
    result = pl.pallas_call(
        functools.partial(kernel, (pools, slabs, points, bands)),
        out_shape=jax.ShapeDtypeStruct((rows, wide), F32),
        in_specs=[vmem] * 10,
        out_specs=vmem,
        scratch_shapes=[
            pltpu.VMEM((slabs, 2 * rows, points), BF16),
            pltpu.VMEM((points, wide), BF16),
            pltpu.VMEM((2 * MODES * rows, points), BF16),
            pltpu.VMEM((slabs, 2 * rows, GROUPS * count), F32),
            pltpu.VMEM((slabs, 2 * rows, GROUPS * count), F32),
            pltpu.VMEM((2, rows, GROUPS * count), F32),
            pltpu.VMEM((2, bands, GROUPS * count), F32),
            pltpu.VMEM((2, rows, GROUPS * count), F32),
            pltpu.VMEM((2 * MODES * rows, GROUPS * count), F32),
            pltpu.VMEM((rows, wide), F32),
            pltpu.VMEM((slabs, rows, wide), BF16),
            pltpu.VMEM((slabs, rows, wide), BF16),
            pltpu.VMEM((slabs, bands, 2 * MODES * rows), BF16),
            pltpu.VMEM((slabs, bands, 2 * MODES * rows), BF16),
            pltpu.VMEM((rows, wide), F32),
            pltpu.VMEM((slabs, rows, 2 * MODES * rows), BF16),
            pltpu.VMEM((slabs, rows, 2 * MODES * rows), BF16),
            dma((slabs,)),
            dma((slabs,)),
            dma((slabs,)),
            dma((slabs,)),
            dma((slabs,)),
            dma((slabs,)),
            dma,
            dma,
            dma((slabs, slabs)),
            dma((slabs, slabs)),
            dma((slabs,)),
            dma((slabs,)),
        ],
        compiler_params=pltpu.CompilerParams(
            collective_id=0, has_side_effects=True, vmem_limit_bytes=58 << 20
        ),
        name="matrix_elements",
    )(
        turned,
        flat,
        pot_rows,
        pot_rows.T,
        projectors.reshape(GROUPS * count, points),
        mode_vectors.reshape(MODES * 6, atoms),
        coupling_base,
        coupling_change,
        projector_atom.reshape(1, count),
        projector_atom.reshape(count, 1),
    )
    return result.reshape(1, rows, MODES, 2, bands)


def solution(mesh):
    placed = (
        P("ka", "ga", None, None),
        P(None, None, "ga"),
        P(None, None, "ga"),
        P(),
        P(),
        P(),
        P(),
    )
    return jax.shard_map(
        body, mesh=mesh, in_specs=placed, out_specs=P("ka", "ga", None, None, None), check_vma=False
    )
```

time: 263 us -> 102 us (0.39)
  waiting for transfers between devices: 168 us -> 0 us
  Pallas kernels: 0 us -> 87.2 us
  matrix products: 22.9 us -> 0 us
  starting transfers between devices: 17.9 us -> 0 us
  other arithmetic: 16 us -> 0 us
  between operations: 13.8 us -> 0.05 us
  local copies, waits for them, and re-layouts: 23.1 us -> 13.6 us
    pallas_call x0 -> x1, Pallas kernels: none -> 87.2 us  [body(): pl.pallas_call(functools.partial(kernel, (pools, slabs, points, bands)),...]
    psum x1 -> x0, waiting for transfers between devices: 84.8 us -> none  [body(): own_proj = lax.psum(own_part, 'ga')]
    reduce_scatter x1 -> x0, waiting for transfers between devices: 81.9 us -> none  [body(): lax.psum_scatter(jnp.transpose(summed, (1, 2, 0, 3)).astype(jnp.bfloat16)...]
    dot_general x27 -> x0, matrix products: 22.9 us -> none  [the longest x8 6.47 us: contract(): return jnp.einsum('vci,cin->vin', left_side, right_side, precision=highest)]
    ppermute x2 -> x0, starting transfers between devices: 17.9 us -> none  [from_behind(): return lax.ppermute(value, axis, pairs)]
    another operation x2 -> x0, other arithmetic: 7.89 us -> none
    mul x2 -> x0, local copies, waits for them, and re-layouts: 5.8 us -> none  [the longest x1 2.92 us: weight_waves(): pot_real[:, :, None] * wave_real[:, None, :]]
    mul x3 -> x0, other arithmetic: 4.27 us -> none  [the longest x1 2.52 us: weight_waves(): pot_real[:, :, None] * wave_real[:, None, :]]
  transfers between devices with their start and end apart: 4 -> 0, of which waited for: 3 -> 0; matrix products, arithmetic and copies ran while one was open for 16% -> 0% of each run, Pallas kernels for 0% -> 0%
where the time goes in v1:
time: 102 us; the launch traced here: 101 us
  Pallas kernels  87.2 us (85%)
  local copies, waits for them, and re-layouts  13.6 us (13%)
    pallas_call x1, Pallas kernels, body(): pl.pallas_call(functools.partial(kernel, (pools, slabs, points, bands)),...  87.2 us
    unnamed x8, local copies, waits for them, and re-layouts  7.43 us
    convert_element_type x2, local copies, waits for them, and re-layouts, body(): pot_rows = potential_change.reshape(2 * MODES, points).astype(F32)  2.09 us

profile of v1, /device:TPU:6, one launch (start us, length us, event | category | flops | bytes accessed | tf_op | source)
XLA Modules:
  0.0 100.8 jit_solution(3607534710938243284)
XLA Ops:
  0.0 0.8 reshape.27.pot_rows
  0.8 0.0 copy-start.1
  0.8 1.3 %copy.14 = f32[8,2048]{0,1:T(8,128)} copy(f32[8,2048]{1,0:T(8,128)S(1)} %reshape.27.pot_rows) | data formatting | bytes 131072 | tf_op jit(solution)/shard_map/convert_element_type | solution.py:430
  2.1 4.7 %copy.12 = bf16[1,2048,2,256]{1,3,2,0:T(8,128)(2,1)S(1)} copy(bf16[1,2048,2,256]{3,2,1,0:T(2,128)(2,1)} %param.7) | data formatting | bytes 4194304 | tf_op args[0]
  6.8 0.0 copy-done.1
  6.8 0.0 copy-start
  6.9 1.5 %copy.13 = bf16[8,2,32,2048]{3,2,1,0:T(8,128)(2,1)} copy(bf16[8,2,32,2048]{3,2,0,1:T(8,128)(2,1)S(1)} %bitcast.15) | data formatting | bytes 4194304 | tf_op jit(solution)/shard_map/transpose | solution.py:427
  8.3 0.9 copy-done
  9.2 0.0 copy-start.2
  9.2 1.8 %copy.16 = bf16[256,8,2,256]{3,1,2,0:T(8,128)(2,1)} copy(bf16[256,8,2,256]{3,2,1,0:T(2,128)(2,1)S(1)} %bitcast.12) | data formatting | bytes 4194304
  11.0 0.0 copy-done.2
  11.0 0.7 copy.15.atom_col
  11.7 87.2 %matrix_elements.1 = f32[32,2048]{1,0:T(8,128)} custom-call(bf16[8,64,2048]{2,1,0:T(8,128)(2,1)} %bitcast.13, bf16[2048,512]{1,0:T(8,128)(2,1)} %bitcast.14, f32[8,2048]{1,0:T(8,128)} %copy-done.1, f32[2048,8]{1,0:T(8,128)} %bitcast.16, bf16[256,2048]{1,0:T(8,128)(2,1)} %bitcast.17, f32[24,8]{1,0:T(8,128)} %bitcast.18, f32[64,64]{1,0:T(8,128)} %base_ref.1, ...), custom_call_target="tpu_custom_call" | custom-call | tf_op jit(solution)/shard_map/matrix_elements/pallas_call | solution.py:434
  98.9 1.9 %reshape.26 = f32[1,32,4,2,256]{4,3,2,1,0:T(2,128)} reshape(f32[32,2048]{1,0:T(8,128)} %matrix_elements.1) | data formatting | bytes 524288 | tf_op jit(solution)/shard_map/reshape | solution.py:486
Async XLA Ops:
  0.8 6.1 %copy-start.1 = (f32[8,2048]{1,0:T(8,128)}, f32[8,2048]{1,0:T(8,128)S(1)}, u32[]{:S(2)}) copy-start(f32[8,2048]{1,0:T(8,128)S(1)} %reshape.27.pot_rows) | copy-start | bytes 196612
  6.8 2.4 %copy-start = (bf16[1,2048,2,256]{3,2,1,0:T(2,128)(2,1)S(1)}, bf16[1,2048,2,256]{3,2,1,0:T(2,128)(2,1)}, u32[]{:S(2)}) copy-start(bf16[1,2048,2,256]{3,2,1,0:T(2,128)(2,1)} %param.7) | copy-start | bytes 6291460
  9.2 1.8 %copy-start.2 = (s32[64]{0:T(128)S(1)}, s32[64]{0:T(128)}, u32[]{:S(2)}) copy-start(s32[64]{0:T(128)} %param.13) | copy-start | bytes 772

commit v2 on v1

v2 whole, which is shorter than its diff:
```python
import functools

import jax
import jax.numpy as jnp
from jax import lax
from jax.experimental import pallas as pl
from jax.experimental.pallas import tpu as pltpu
from jax.sharding import PartitionSpec as P

MESH = pl.DeviceIdType.MESH
F32 = jnp.float32
BF16 = jnp.bfloat16
HIGHEST = lax.Precision.HIGHEST
MODES = 4
GROUPS = 4
AHEAD = 3
WIDTH = 128


def dot_nn(left, right, precision=None):
    return jnp.dot(left, right, preferred_element_type=F32, precision=precision)


def dot_nt(left, right, precision=None):
    return lax.dot_general(
        left, right, (((1,), (1,)), ((), ())), preferred_element_type=F32, precision=precision
    )


def nonlocal_rows(rows_ref, all_proj, vec_rows, base_ref, change_ref, same, mixed, result):
    count = same.shape[0]
    rows = rows_ref.shape[1]
    base = 0.5 * (base_ref[...] + base_ref[...].T) * same
    conj_re = rows_ref[0]
    conj_im = -rows_ref[1]

    def group(value, j):
        return value[:, j * count : (j + 1) * count]

    def vec(mode, c):
        at = (mode * 3 + c) * 2
        return vec_rows[at : at + 1, :], vec_rows[at + 1 : at + 2, :]

    bra = []
    for mode in range(MODES):
        total_re = jnp.zeros((rows, count), F32)
        total_im = jnp.zeros((rows, count), F32)
        for c in range(3):
            v_re, v_im = vec(mode, c)
            g_re, g_im = group(conj_re, c + 1), group(conj_im, c + 1)
            total_re = total_re - (v_re * g_re - v_im * g_im)
            total_im = total_im - (v_re * g_im + v_im * g_re)
        bra += [total_re, total_im]
    bra_base = dot_nn(jnp.concatenate(bra, axis=0), base, HIGHEST)
    value = jnp.concatenate([group(conj_re, 0), group(conj_im, 0)], axis=0)
    value_base = dot_nn(value, base, HIGHEST)
    t_re, t_im = value_base[:rows], value_base[rows:]
    for mode in range(MODES):
        with_re = dot_nn(value, change_ref[mode, 0] * same, HIGHEST)
        with_im = dot_nn(value, change_ref[mode, 1] * same, HIGHEST)
        at = mode * 2 * rows
        mixed[at : at + rows, 0:count] = bra_base[at : at + rows] + with_re[:rows] - with_im[rows:]
        mixed[at + rows : at + 2 * rows, 0:count] = (
            bra_base[at + rows : at + 2 * rows] + with_im[:rows] + with_re[rows:]
        )
        for c in range(3):
            v_re, v_im = vec(mode, c)
            lanes = slice((c + 1) * count, (c + 2) * count)
            mixed[at : at + rows, lanes] = -(t_re * v_re - t_im * v_im)
            mixed[at + rows : at + 2 * rows, lanes] = -(t_re * v_im + t_im * v_re)
    by_re = dot_nt(mixed[...], all_proj[0], HIGHEST)
    by_im = dot_nt(mixed[...], all_proj[1], HIGHEST)
    bands = by_re.shape[1]
    for mode in range(MODES):
        at = mode * 2 * rows
        re, im = slice(at, at + rows), slice(at + rows, at + 2 * rows)
        lane = mode * 2 * bands
        result[:, lane : lane + bands] = by_re[re] - by_im[im]
        result[:, lane + bands : lane + 2 * bands] = by_im[re] + by_re[im]


def kernel(
    sizes,
    wave_in,
    pot_in,
    projectors_in,
    vec_in,
    base_in,
    change_in,
    atom_in,
    out_ref,
    raw,
    pot_raw,
    projectors,
    vec_ref,
    base_ref,
    change_ref,
    atom_row,
    pick,
    pot_rows,
    turned,
    flat,
    landing,
    weighted,
    weighted_t,
    proj_part,
    proj_x,
    proj_send,
    proj_y,
    proj_own,
    all_proj,
    rows_land,
    mixed,
    nonlocal_sum,
    sum_send,
    sum_land,
    held,
    pair_send,
    pair_land,
    piece_send,
    piece_land,
    piece_held,
    half_send,
    half_land,
    back_send,
    back_land,
    last_send,
    last_land,
    stream_sems,
    proj_x_sems,
    gather_sems,
    lone_sems,
    sum_sems,
    piece_sems,
    half_sems,
    back_sems,
    local_sems,
):
    pools, slabs, points, bands = sizes
    rows = bands // slabs
    across = slabs // 2
    step = pools // 4
    ka = lax.axis_index("ka")
    ga = lax.axis_index("ga")
    core = lax.rem(ka, 2)
    x = ga // 2
    half = lax.rem(ga, 2)
    ahead_k = lax.rem(ka + step, pools)
    behind_k = lax.rem(ka + pools - step, pools)

    def x_peer(d):
        return lax.rem(x + d, across)

    def at_x(d):
        return (ka, x_peer(d) * 2 + half)

    other = x * 2 + 1 - half
    other_half = (ka, other)

    def remote(src, dst, sems, where):
        return pltpu.make_async_remote_copy(
            src_ref=src,
            dst_ref=dst,
            send_sem=sems[0],
            recv_sem=sems[1],
            device_id=where,
            device_id_type=MESH,
        )

    def rows_of(first, count):
        return pl.ds(pl.multiple_of(first, count), count)

    barrier = pltpu.get_barrier_semaphore()
    peers = [at_x(d) for d in range(1, across)] + [other_half]
    peers += [(k, g) for k in (ahead_k, behind_k) for g in (ga, other)]
    for where in peers:
        pl.semaphore_signal(barrier, inc=1, device_id=where, device_id_type=MESH)

    first_half = jnp.where(core == 0, 0, x_peer(1) // 2)

    def fetch_wave(h):
        lanes = pl.ds(pl.multiple_of(h * WIDTH, WIDTH), WIDTH)
        return pltpu.make_async_copy(wave_in.at[:, :, lanes], raw.at[h], local_sems.at[h])

    fetches = [
        pltpu.make_async_copy(src, dst, local_sems.at[2 + i])
        for i, (src, dst) in enumerate(
            (
                (pot_in, pot_raw),
                (projectors_in, projectors),
                (vec_in, vec_ref),
                (base_in, base_ref),
                (change_in, change_ref),
                (atom_in, atom_row),
            )
        )
    ]
    fetch_wave(first_half).start()
    fetch_wave(1 - first_half).start()
    for fetch in fetches:
        fetch.start()
    row = lax.broadcasted_iota(jnp.int32, pick.shape, 0)
    column = lax.broadcasted_iota(jnp.int32, pick.shape, 1)
    part = (row >= WIDTH).astype(jnp.int32)
    pick[...] = (column == 2 * (row - WIDTH * part) + part).astype(BF16)
    paired = raw.reshape(2, 2 * points, WIDTH)

    def turn(h):
        fetch_wave(h).wait()
        chunks = WIDTH // rows

        def block(b, carry):
            here = rows_of(b * WIDTH, WIDTH)
            planes = dot_nn(pick[...], paired[h, rows_of(b * 2 * WIDTH, 2 * WIDTH), :]).astype(BF16)
            for c in range(2):
                plane = planes[c * WIDTH : (c + 1) * WIDTH]
                flat[here, pl.ds(pl.multiple_of(c * bands + h * WIDTH, WIDTH), WIDTH)] = plane
                across_points = plane.T
                for j in range(chunks):
                    turned[h * chunks + j, c * rows : (c + 1) * rows, here] = across_points[
                        j * rows : (j + 1) * rows
                    ]
            return carry

        lax.fori_loop(0, points // WIDTH, block, 0, unroll=4)

    turn(first_half)
    pl.semaphore_wait(barrier, len(peers))

    target_k = jnp.where(core == 0, ahead_k, behind_k)

    def stream(s):
        place = lax.rem(x + 1 + lax.rem(s, across), across) * 2
        side = jnp.where(s < across, 1 - half, half)
        chunk = jnp.where(core == 0, s, place + side)
        return remote(
            turned.at[chunk],
            landing.at[s],
            (stream_sems.at[0, s], stream_sems.at[1, s]),
            (target_k, ga),
        )

    stream(0).start()
    turn(1 - first_half)
    for s in range(1, AHEAD):
        stream(s).start()
    for fetch in fetches:
        fetch.wait()

    turned_rows = turned.reshape(slabs * 2 * rows, points)
    proj_part[...] = dot_nt(turned_rows[...], projectors[...]).reshape(proj_part.shape)

    def proj_x_copy(d):
        return remote(
            proj_part.at[pl.ds(x_peer(d) * 2, 2)],
            proj_x.at[d - 1],
            (proj_x_sems.at[0, d], proj_x_sems.at[1, d]),
            at_x(d),
        )

    for d in range(1, across):
        proj_x_copy(d).start()

    for mode in range(MODES):
        pot_rows[2 * mode : 2 * mode + 2, :] = pot_raw[mode].astype(F32)

    @pl.when(core == 1)
    def _():
        block = 128

        def weigh(i, carry):
            at = pl.ds(pl.multiple_of(i * block, block), block)
            re = flat[at, 0:bands].astype(F32)
            im = flat[at, bands : 2 * bands].astype(F32)
            cols = pot_rows[:, at].T
            for mode in range(MODES):
                p_re = cols[:, 2 * mode : 2 * mode + 1]
                p_im = cols[:, 2 * mode + 1 : 2 * mode + 2]
                lane = mode * 2 * bands
                weighted[at, lane : lane + bands] = (p_re * re - p_im * im).astype(BF16)
                weighted[at, lane + bands : lane + 2 * bands] = (p_re * im + p_im * re).astype(BF16)
            return carry

        lax.fori_loop(0, points // block, weigh, 0)

    proj_y_copy = remote(proj_send, proj_y, (lone_sems.at[0], lone_sems.at[1]), other_half)
    own_rows = rows_of(ga * rows, rows)
    pair_rows = rows_of(x * 2 * rows, 2 * rows)
    gather_y = remote(
        proj_own,
        all_proj.at[:, own_rows, :],
        (lone_sems.at[2], lone_sems.at[3]),
        other_half,
    )
    gather_y_arrival = remote(
        proj_own,
        all_proj.at[:, rows_of((x * 2 + 1 - half) * rows, rows), :],
        (lone_sems.at[2], lone_sems.at[3]),
        other_half,
    )
    rows_copy = remote(
        proj_own, rows_land, (lone_sems.at[4], lone_sems.at[5]), (behind_k, ga)
    )

    def gather_x(d, first):
        block = rows_of(first * 2 * rows, 2 * rows)
        return remote(
            all_proj.at[:, block, :],
            all_proj.at[:, block, :],
            (gather_sems.at[0, d], gather_sems.at[1, d]),
            at_x(d),
        )

    def proj_sum(side):
        value = proj_part[x * 2 + side]
        for d in range(1, across):
            value = value + proj_x[d - 1, side]
        return value

    def proj_stage_0():
        for d in range(1, across):
            proj_x_copy(d).wait_recv()
        proj_send[...] = proj_sum(1 - half)
        proj_y_copy.start()

    def proj_stage_1():
        proj_y_copy.wait_recv()
        value = proj_sum(half) + proj_y[...]
        proj_own[0] = value[:rows]
        proj_own[1] = value[rows:]
        rows_copy.start()
        gather_y.start()
        all_proj[0, own_rows, :] = value[:rows]
        all_proj[1, own_rows, :] = value[rows:]

    def proj_stage_2():
        gather_y_arrival.wait_recv()
        for d in range(1, across):
            gather_x(d, x).start()

    def nonlocal_part():
        for d in range(1, across):
            gather_x(d, x_peer(across - d)).wait_recv()
        rows_copy.wait_recv()
        atoms = vec_ref.shape[1]
        onehot = (
            lax.broadcasted_iota(jnp.int32, (atoms, atom_row.shape[1]), 0) == atom_row[...]
        ).astype(F32)
        vec_rows = dot_nn(vec_ref[...], onehot, HIGHEST)
        same = dot_nn(onehot.T, onehot)
        nonlocal_rows(
            rows_land, all_proj, vec_rows, base_ref, change_ref, same, mixed, nonlocal_sum
        )

    def next_chunk(s):
        stream(s).wait_recv()
        stream(s).wait_send()

        @pl.when(s + AHEAD < slabs)
        def _():
            stream(s + AHEAD).start()

    def beside(s):
        for at, stage in enumerate((proj_stage_1, proj_stage_2, None, nonlocal_part)):
            if stage is not None:
                pl.when(s == at)(stage)

    proj_stage_0()

    @pl.when(core == 1)
    def _():
        def sum_copy(s):
            return remote(
                sum_send.at[s],
                sum_land.at[s],
                (sum_sems.at[0, s], sum_sems.at[1, s]),
                at_x(1 + lax.rem(s, across)),
            )

        pair_copy = remote(pair_send, pair_land, (lone_sems.at[6], lone_sems.at[7]), other_half)

        def chunk_sum(s, put):
            for mode in range(MODES):
                lane = mode * 2 * bands
                both = dot_nn(landing[s], weighted[:, lane : lane + 2 * bands])
                put(lane, both[:rows, :bands] + both[rows:, bands:])
                put(lane + bands, both[:rows, bands:] - both[rows:, :bands])

        def arrived(first, lane):
            value = held[:, lane : lane + bands]
            for s in range(first, first + across - 1):
                value = value + sum_land[s, :, lane : lane + bands].astype(F32)
            return value

        def one(s, carry):
            next_chunk(s)
            kept = lax.rem(s, across) == across - 1

            def put_send(lane, value):
                sum_send[s, :, lane : lane + bands] = value.astype(BF16)

            def put_held(lane, value):
                held[:, lane : lane + bands] = value

            @pl.when(kept)
            def _():
                chunk_sum(s, put_held)

            @pl.when(jnp.logical_not(kept))
            def _():
                chunk_sum(s, put_send)
                sum_copy(s).start()

            @pl.when(s == across)
            def _():
                for i in range(across - 1):
                    sum_copy(i).wait_recv()
                for lane in range(0, 2 * MODES * bands, bands):
                    pair_send[:, lane : lane + bands] = arrived(0, lane).astype(BF16)
                pair_copy.start()

            beside(s)
            return carry

        lax.fori_loop(0, slabs, one, 0)
        pair_copy.wait_recv()
        for i in range(across, slabs - 1):
            sum_copy(i).wait_recv()
        for i in range(2 * MODES):
            here = slice(i * bands, (i + 1) * bands)
            out_ref[:, i // 2, i % 2, :] = (
                arrived(across, i * bands) + pair_land[:, here].astype(F32) + nonlocal_sum[:, here]
            )
        for s in list(range(across - 1)) + list(range(across, slabs - 1)):
            sum_copy(s).wait_send()
        pair_copy.wait_send()

    @pl.when(core == 0)
    def _():
        def piece_copy(s, d):
            return remote(
                piece_send.at[s, rows_of(x_peer(d) * 2 * rows, 2 * rows)],
                piece_land.at[s, pl.ds((d - 1) * 2 * rows, 2 * rows)],
                (piece_sems.at[0, s, d], piece_sems.at[1, s, d]),
                at_x(d),
            )

        def half_copy(s):
            return remote(
                half_send.at[s],
                half_land.at[s],
                (half_sems.at[0, s], half_sems.at[1, s]),
                other_half,
            )

        def back_copy(s):
            return remote(
                back_send.at[s],
                back_land.at[s],
                (back_sems.at[0, s], back_sems.at[1, s]),
                (behind_k, ga),
            )

        def last_copy(side):
            return remote(
                last_send.at[side],
                last_land.at[side],
                (lone_sems.at[8 + 2 * side], lone_sems.at[9 + 2 * side]),
                (behind_k, ga if side == 0 else other),
            )

        def chunk_sum(s):
            block = 512
            for at in range(0, points, block):
                re = landing[s, 0:rows, at : at + block].astype(F32)
                im = landing[s, rows : 2 * rows, at : at + block].astype(F32)
                for mode in range(MODES):
                    p_re = pot_rows[2 * mode : 2 * mode + 1, at : at + block]
                    p_im = pot_rows[2 * mode + 1 : 2 * mode + 2, at : at + block]
                    top = mode * rows
                    weighted_t[top : top + rows, at : at + block] = (p_re * re - p_im * im).astype(
                        BF16
                    )
                    top = (MODES + mode) * rows
                    weighted_t[top : top + rows, at : at + block] = (p_re * im + p_im * re).astype(
                        BF16
                    )
            both = dot_nn(weighted_t[...], flat[...])
            many = MODES * rows
            real = both[:many, :bands] + both[many:, bands:]
            imag = both[many:, :bands] - both[:many, bands:]
            piece_send[s, :, 0:many] = real.T.astype(BF16)
            piece_send[s, :, many : 2 * many] = imag.T.astype(BF16)
            for d in range(1, across):
                piece_copy(s, d).start()

        def total(s, side):
            first = pl.multiple_of((x * 2 + side) * rows, rows)
            value = piece_send[s, pl.ds(first, rows)].astype(F32)
            for d in range(1, across):
                first = pl.multiple_of(((d - 1) * 2 + side) * rows, rows)
                value = value + piece_land[s, pl.ds(first, rows)].astype(F32)
            return value

        def reduce_x(s):
            for d in range(1, across):
                piece_copy(s, d).wait_recv()
            half_send[s] = total(s, 1 - half).astype(BF16)
            half_copy(s).start()
            piece_held[s] = total(s, half)

        def reduce_y(s):
            half_copy(s).wait_recv()
            back_send[s] = (piece_held[s] + half_land[s].astype(F32)).astype(BF16)
            back_copy(s).start()

        def one(s, carry):
            next_chunk(s)
            chunk_sum(s)

            @pl.when(s >= 1)
            def _():
                reduce_x(s - 1)

            @pl.when(s >= 2)
            def _():
                reduce_y(s - 2)

            beside(s)
            return carry

        lax.fori_loop(0, slabs, one, 0)
        for d in range(1, across):
            piece_copy(slabs - 1, d).wait_recv()
        for side in range(2):
            last_send[side] = total(slabs - 1, half if side == 0 else 1 - half).astype(BF16)
            last_copy(side).start()
        reduce_y(slabs - 2)
        for s in range(slabs - 1):
            back_copy(s).wait_recv()
        for side in range(2):
            last_copy(side).wait_recv()
        per = WIDTH // rows
        at_lane = lax.broadcasted_iota(jnp.int32, (rows, WIDTH), 1)

        def summed(chunk, part):
            here = slice(part * WIDTH, (part + 1) * WIDTH)
            if chunk < slabs - 1:
                return back_land[chunk, :, here].astype(F32)
            return last_land[0, :, here].astype(F32) + last_land[1, :, here].astype(F32)

        for mode in range(MODES):
            for part in range(2):
                for q in range(bands // WIDTH):
                    value = jnp.zeros((rows, WIDTH), F32)
                    for t in range(per):
                        piece = summed(q * per + t, part)
                        shift = (t - mode) * rows % WIDTH
                        if shift:
                            piece = pltpu.roll(piece, shift, 1)
                        inside = (at_lane >= t * rows) & (at_lane < (t + 1) * rows)
                        value = jnp.where(inside, piece, value)
                    lane = (mode * 2 + part) * bands + q * WIDTH
                    out_ref[:, mode, part, q * WIDTH : (q + 1) * WIDTH] = (
                        value + nonlocal_sum[:, lane : lane + WIDTH]
                    )
        for s in range(slabs):
            if s < slabs - 1:
                back_copy(s).wait_send()
                half_copy(s).wait_send()
            else:
                last_copy(0).wait_send()
                last_copy(1).wait_send()
            for d in range(1, across):
                piece_copy(s, d).wait_send()

    for d in range(1, across):
        proj_x_copy(d).wait_send()
        gather_x(d, x).wait_send()
    proj_y_copy.wait_send()
    gather_y.wait_send()
    rows_copy.wait_send()


def body(
    wave_fields,
    potential_change,
    projectors,
    mode_vectors,
    coupling_base,
    coupling_change,
    projector_atom,
):
    own = wave_fields[0]
    points, _, bands = own.shape
    pools, slabs = lax.axis_size("ka"), lax.axis_size("ga")
    count = projectors.shape[1]
    atoms = mode_vectors.shape[-1]
    rows = bands // slabs
    across = slabs // 2
    columns = GROUPS * count
    wide = 2 * MODES * bands
    part_wide = 2 * MODES * rows
    vmem = pl.BlockSpec(memory_space=pltpu.VMEM)
    dma = pltpu.SemaphoreType.DMA
    result = pl.pallas_call(
        functools.partial(kernel, (pools, slabs, points, bands)),
        out_shape=jax.ShapeDtypeStruct((rows, MODES, 2, bands), F32),
        in_specs=[pl.BlockSpec(memory_space=pl.ANY)] * 7,
        out_specs=vmem,
        scratch_shapes=[
            pltpu.VMEM((bands // WIDTH, points, 2, WIDTH), BF16),
            pltpu.VMEM(potential_change.shape, BF16),
            pltpu.VMEM((columns, points), BF16),
            pltpu.VMEM((MODES * 6, atoms), F32),
            pltpu.VMEM(coupling_base.shape, F32),
            pltpu.VMEM(coupling_change.shape, F32),
            pltpu.VMEM((1, count), jnp.int32),
            pltpu.VMEM((2 * WIDTH, 2 * WIDTH), BF16),
            pltpu.VMEM((2 * MODES, points), F32),
            pltpu.VMEM((slabs, 2 * rows, points), BF16),
            pltpu.VMEM((points, 2 * bands), BF16),
            pltpu.VMEM((slabs, 2 * rows, points), BF16),
            pltpu.VMEM((points, wide), BF16),
            pltpu.VMEM((2 * MODES * rows, points), BF16),
            pltpu.VMEM((slabs, 2 * rows, columns), F32),
            pltpu.VMEM((across - 1, 2, 2 * rows, columns), F32),
            pltpu.VMEM((2 * rows, columns), F32),
            pltpu.VMEM((2 * rows, columns), F32),
            pltpu.VMEM((2, rows, columns), F32),
            pltpu.VMEM((2, bands, columns), F32),
            pltpu.VMEM((2, rows, columns), F32),
            pltpu.VMEM((2 * MODES * rows, columns), F32),
            pltpu.VMEM((rows, wide), F32),
            pltpu.VMEM((slabs, rows, wide), BF16),
            pltpu.VMEM((slabs, rows, wide), BF16),
            pltpu.VMEM((rows, wide), F32),
            pltpu.VMEM((rows, wide), BF16),
            pltpu.VMEM((rows, wide), BF16),
            pltpu.VMEM((slabs, bands, part_wide), BF16),
            pltpu.VMEM((slabs, (across - 1) * 2 * rows, part_wide), BF16),
            pltpu.VMEM((slabs, rows, part_wide), F32),
            pltpu.VMEM((slabs, rows, part_wide), BF16),
            pltpu.VMEM((slabs, rows, part_wide), BF16),
            pltpu.VMEM((slabs, rows, part_wide), BF16),
            pltpu.VMEM((slabs, rows, part_wide), BF16),
            pltpu.VMEM((2, rows, part_wide), BF16),
            pltpu.VMEM((2, rows, part_wide), BF16),
            dma((2, slabs)),
            dma((2, across)),
            dma((2, across)),
            dma((12,)),
            dma((2, slabs)),
            dma((2, slabs, across)),
            dma((2, slabs)),
            dma((2, slabs)),
            dma((8,)),
        ],
        compiler_params=pltpu.CompilerParams(
            collective_id=0, has_side_effects=True, vmem_limit_bytes=58 << 20
        ),
        name="matrix_elements",
    )(
        own,
        potential_change,
        projectors.reshape(columns, points),
        mode_vectors.reshape(MODES * 6, atoms),
        coupling_base,
        coupling_change,
        projector_atom.reshape(1, count),
    )
    return result[None]


def solution(mesh):
    placed = (
        P("ka", "ga", None, None),
        P(None, None, "ga"),
        P(None, None, "ga"),
        P(),
        P(),
        P(),
        P(),
    )
    return jax.shard_map(
        body, mesh=mesh, in_specs=placed, out_specs=P("ka", "ga", None, None, None), check_vma=False
    )
```

time: 102 us -> 79.3 us (0.78)
  the two profiles are of different devices: /device:TPU:6 before, /device:TPU:16 now
where the time goes in v2:
time: 79.3 us; the launch traced here: 79.1 us
  Pallas kernels  77.5 us (98%)
  local copies, waits for them, and re-layouts  1.67 us (2%)
    pallas_call x1, Pallas kernels, body(): pl.pallas_call(functools.partial(kernel, (pools, slabs, points, bands)),...  77.5 us
    unnamed x1, local copies, waits for them, and re-layouts  1.67 us

profile of v2, /device:TPU:16, one launch (start us, length us, event | category | flops | bytes accessed | tf_op | source)
XLA Modules:
  0.0 79.1 jit_solution(14241803250833433742)
XLA Ops:
  0.0 77.5 %matrix_elements.1 = f32[32,4,2,256]{3,2,1,0:T(2,128)} custom-call(bf16[2048,2,256]{2,1,0:T(2,128)(2,1)} %bitcast.5, bf16[4,2,2048]{2,1,0:T(2,128)(2,1)} %pot_in.1, bf16[256,2048]{1,0:T(8,128)(2,1)} %bitcast.6, f32[24,8]{1,0:T(8,128)} %bitcast.8, f32[64,64]{1,0:T(8,128)} %base_in.1, f32[4,2,64,64]{3,2,1,0:T(8,128)} %change_in.1, s32[1,64]{1,0:T(1,128)} %bitcast.9), custom_call_target="tpu_custom_call" | custom-call | tf_op jit(solution)/shard_map/matrix_elements/pallas_call | solution.py:606
  77.5 1.7 %copy.9 = f32[1,32,4,2,256]{4,3,2,1,0:T(2,128)} copy(f32[1,32,4,2,256]{4,3,2,1,0:T(2,128)} %bitcast.7) | data formatting | bytes 524288

commit v3 on v2

--- a/solution.py
+++ b/solution.py
@@ -14,7 +14,12 @@
 MODES = 4
 GROUPS = 4
 AHEAD = 3
+SLACK = 1
+QUARTERS = 4
 WIDTH = 128
+STAGES = (1, 2, 3, 5)
+LAG_X, LAG_Y = 1, 3
+DIRECT = 2
 
 
 def dot_nn(left, right, precision=None):
@@ -126,6 +131,9 @@
     back_land,
     last_send,
     last_land,
+    home_land,
+    sums,
+    sums_t,
     stream_sems,
     proj_x_sems,
     gather_sems,
@@ -134,7 +142,11 @@
     piece_sems,
     half_sems,
     back_sems,
+    last_sems,
+    home_sems,
     local_sems,
+    raw_sems,
+    paces,
 ):
     pools, slabs, points, bands = sizes
     rows = bands // slabs
@@ -172,18 +184,25 @@
 
     barrier = pltpu.get_barrier_semaphore()
     peers = [at_x(d) for d in range(1, across)] + [other_half]
-    peers += [(k, g) for k in (ahead_k, behind_k) for g in (ga, other)]
+    peers += [(k, lax.rem(ga + d, slabs)) for k in (ahead_k, behind_k) for d in range(slabs)]
+    between = [(lax.rem(ka + d, pools), ga) for d in (step // 2, pools - step // 2)]
+    peers += between
     for where in peers:
         pl.semaphore_signal(barrier, inc=1, device_id=where, device_id_type=MESH)
 
     first_half = jnp.where(core == 0, 0, x_peer(1) // 2)
 
-    def fetch_wave(h):
+    quarter = points // QUARTERS
+
+    def fetch_wave(h, q):
         lanes = pl.ds(pl.multiple_of(h * WIDTH, WIDTH), WIDTH)
-        return pltpu.make_async_copy(wave_in.at[:, :, lanes], raw.at[h], local_sems.at[h])
+        here = pl.ds(q * quarter, quarter)
+        return pltpu.make_async_copy(
+            wave_in.at[here, :, lanes], raw.at[h, here], raw_sems.at[h, q]
+        )
 
     fetches = [
-        pltpu.make_async_copy(src, dst, local_sems.at[2 + i])
+        pltpu.make_async_copy(src, dst, local_sems.at[i])
         for i, (src, dst) in enumerate(
             (
                 (pot_in, pot_raw),
@@ -195,8 +214,9 @@
             )
         )
     ]
-    fetch_wave(first_half).start()
-    fetch_wave(1 - first_half).start()
+    for h in (first_half, 1 - first_half):
+        for q in range(QUARTERS):
+            fetch_wave(h, q).start()
     for fetch in fetches:
         fetch.start()
     row = lax.broadcasted_iota(jnp.int32, pick.shape, 0)
@@ -205,8 +225,8 @@
     pick[...] = (column == 2 * (row - WIDTH * part) + part).astype(BF16)
     paired = raw.reshape(2, 2 * points, WIDTH)
 
-    def turn(h):
-        fetch_wave(h).wait()
+    def turn(h, q):
+        fetch_wave(h, q).wait()
         chunks = WIDTH // rows
 
         def block(b, carry):
@@ -222,26 +242,38 @@
                     ]
             return carry
 
-        lax.fori_loop(0, points // WIDTH, block, 0, unroll=4)
-
-    turn(first_half)
+        blocks = quarter // WIDTH
+        lax.fori_loop(q * blocks, (q + 1) * blocks, block, 0, unroll=True)
+
+    turn(first_half, 0)
     pl.semaphore_wait(barrier, len(peers))
 
     target_k = jnp.where(core == 0, ahead_k, behind_k)
 
-    def stream(s):
+    final = slabs - 1
+    quarters = [pl.ds(q * quarter, quarter) for q in range(QUARTERS)]
+
+    def stream(s, points_here=slice(None), sem=None):
         place = lax.rem(x + 1 + lax.rem(s, across), across) * 2
         side = jnp.where(s < across, 1 - half, half)
         chunk = jnp.where(core == 0, s, place + side)
+        sem = s if sem is None else sem
         return remote(
-            turned.at[chunk],
-            landing.at[s],
-            (stream_sems.at[0, s], stream_sems.at[1, s]),
+            turned.at[chunk, :, points_here],
+            landing.at[s, :, points_here],
+            (stream_sems.at[0, sem], stream_sems.at[1, sem]),
             (target_k, ga),
         )
 
-    stream(0).start()
-    turn(1 - first_half)
+    def last_quarter(q):
+        return stream(final, quarters[q], final + q)
+
+    for q, here in enumerate(quarters):
+        if q:
+            turn(first_half, q)
+        stream(0, here).start()
+    for q in range(QUARTERS):
+        turn(1 - first_half, q)
     for s in range(1, AHEAD):
         stream(s).start()
     for fetch in fetches:
@@ -354,18 +386,28 @@
 
     def next_chunk(s):
         stream(s).wait_recv()
+        for i, where in enumerate(between):
+            pl.semaphore_signal(paces.at[i], inc=1, device_id=where, device_id_type=MESH)
         stream(s).wait_send()
 
-        @pl.when(s + AHEAD < slabs)
+        @pl.when(jnp.logical_and(s + AHEAD <= final, s >= SLACK))
+        def _():
+            for i in range(2):
+                pl.semaphore_wait(paces.at[i], 1)
+
+        @pl.when(s + AHEAD < final)
         def _():
             stream(s + AHEAD).start()
 
+        @pl.when(s + AHEAD == final)
+        def _():
+            for q in range(QUARTERS):
+                last_quarter(q).start()
+
     def beside(s):
-        for at, stage in enumerate((proj_stage_1, proj_stage_2, None, nonlocal_part)):
-            if stage is not None:
-                pl.when(s == at)(stage)
-
-    proj_stage_0()
+        stages = (proj_stage_0, proj_stage_1, proj_stage_2, nonlocal_part)
+        for at, stage in zip(STAGES, stages):
+            pl.when(s == at)(stage)
 
     @pl.when(core == 1)
     def _():
@@ -379,12 +421,14 @@
 
         pair_copy = remote(pair_send, pair_land, (lone_sems.at[6], lone_sems.at[7]), other_half)
 
+        def parts_of(both, lane, put):
+            put(lane, both[:rows, :bands] + both[rows:, bands:])
+            put(lane + bands, both[:rows, bands:] - both[rows:, :bands])
+
         def chunk_sum(s, put):
-            for mode in range(MODES):
-                lane = mode * 2 * bands
+            for lane in range(0, 2 * MODES * bands, 2 * bands):
                 both = dot_nn(landing[s], weighted[:, lane : lane + 2 * bands])
-                put(lane, both[:rows, :bands] + both[rows:, bands:])
-                put(lane + bands, both[:rows, bands:] - both[rows:, :bands])
+                parts_of(both, lane, put)
 
         def arrived(first, lane):
             value = held[:, lane : lane + bands]
@@ -392,15 +436,15 @@
                 value = value + sum_land[s, :, lane : lane + bands].astype(F32)
             return value
 
+        def put_held(lane, value):
+            held[:, lane : lane + bands] = value
+
         def one(s, carry):
             next_chunk(s)
-            kept = lax.rem(s, across) == across - 1
+            kept = s == across - 1
 
             def put_send(lane, value):
                 sum_send[s, :, lane : lane + bands] = value.astype(BF16)
-
-            def put_held(lane, value):
-                held[:, lane : lane + bands] = value
 
             @pl.when(kept)
             def _():
@@ -422,7 +466,17 @@
             beside(s)
             return carry
 
-        lax.fori_loop(0, slabs, one, 0)
+        lax.fori_loop(0, final, one, 0)
+        for q, here in enumerate(quarters):
+            last_quarter(q).wait_recv()
+            for lane in range(0, 2 * MODES * bands, 2 * bands):
+                lanes = slice(lane, lane + 2 * bands)
+                both = dot_nn(landing[final, :, here], weighted[here, lanes])
+                both = both if q == 0 else sums[:, lanes] + both
+                if q < QUARTERS - 1:
+                    sums[:, lanes] = both
+                else:
+                    parts_of(both, lane, put_held)
         pair_copy.wait_recv()
         for i in range(across, slabs - 1):
             sum_copy(i).wait_recv()
@@ -461,38 +515,43 @@
                 (behind_k, ga),
             )
 
-        def last_copy(side):
+        passed = final - DIRECT
+
+        def last_copy(i, side):
             return remote(
-                last_send.at[side],
-                last_land.at[side],
-                (lone_sems.at[8 + 2 * side], lone_sems.at[9 + 2 * side]),
+                last_send.at[i, side],
+                last_land.at[i, side],
+                (last_sems.at[0, i, side], last_sems.at[1, i, side]),
                 (behind_k, ga if side == 0 else other),
             )
 
-        def chunk_sum(s):
-            block = 512
-            for at in range(0, points, block):
-                re = landing[s, 0:rows, at : at + block].astype(F32)
-                im = landing[s, rows : 2 * rows, at : at + block].astype(F32)
-                for mode in range(MODES):
-                    p_re = pot_rows[2 * mode : 2 * mode + 1, at : at + block]
-                    p_im = pot_rows[2 * mode + 1 : 2 * mode + 2, at : at + block]
-                    top = mode * rows
-                    weighted_t[top : top + rows, at : at + block] = (p_re * re - p_im * im).astype(
-                        BF16
-                    )
-                    top = (MODES + mode) * rows
-                    weighted_t[top : top + rows, at : at + block] = (p_re * im + p_im * re).astype(
-                        BF16
-                    )
-            both = dot_nn(weighted_t[...], flat[...])
-            many = MODES * rows
+        def home_copy(d):
+            peer = lax.rem(ga + d, slabs)
+            return remote(
+                piece_send.at[final, rows_of(peer * rows, rows)],
+                home_land.at[d],
+                (home_sems.at[0, d], home_sems.at[1, d]),
+                (behind_k, peer),
+            )
+
+        many = MODES * rows
+
+        def weigh_turned(s, here):
+            re = landing[s, 0:rows, here].astype(F32)
+            im = landing[s, rows : 2 * rows, here].astype(F32)
+            for mode in range(MODES):
+                p_re = pot_rows[2 * mode : 2 * mode + 1, here]
+                p_im = pot_rows[2 * mode + 1 : 2 * mode + 2, here]
+                top = mode * rows
+                weighted_t[top : top + rows, here] = (p_re * re - p_im * im).astype(BF16)
+                top = many + mode * rows
+                weighted_t[top : top + rows, here] = (p_re * im + p_im * re).astype(BF16)
+
+        def pieces(s, both):
             real = both[:many, :bands] + both[many:, bands:]
             imag = both[many:, :bands] - both[:many, bands:]
             piece_send[s, :, 0:many] = real.T.astype(BF16)
             piece_send[s, :, many : 2 * many] = imag.T.astype(BF16)
-            for d in range(1, across):
-                piece_copy(s, d).start()
 
         def total(s, side):
             first = pl.multiple_of((x * 2 + side) * rows, rows)
@@ -505,9 +564,20 @@
         def reduce_x(s):
             for d in range(1, across):
                 piece_copy(s, d).wait_recv()
-            half_send[s] = total(s, 1 - half).astype(BF16)
-            half_copy(s).start()
-            piece_held[s] = total(s, half)
+
+            @pl.when(s < passed)
+            def _():
+                half_send[s] = total(s, 1 - half).astype(BF16)
+                half_copy(s).start()
+                piece_held[s] = total(s, half)
+
+            @pl.when(s >= passed)
+            def _():
+                for side in range(2):
+                    last_send[s - passed, side] = total(s, half if side == 0 else 1 - half).astype(
+                        BF16
+                    )
+                    last_copy(s - passed, side).start()
 
         def reduce_y(s):
             half_copy(s).wait_recv()
@@ -516,38 +586,59 @@
 
         def one(s, carry):
             next_chunk(s)
-            chunk_sum(s)
-
-            @pl.when(s >= 1)
+            for here in quarters:
+                weigh_turned(s, here)
+            pieces(s, dot_nn(weighted_t[...], flat[...]))
+            for d in range(1, across):
+                piece_copy(s, d).start()
+
+            @pl.when(s >= LAG_X)
             def _():
-                reduce_x(s - 1)
-
-            @pl.when(s >= 2)
+                reduce_x(s - LAG_X)
+
+            @pl.when(jnp.logical_and(s >= LAG_Y, s < passed + LAG_Y))
             def _():
-                reduce_y(s - 2)
+                reduce_y(s - LAG_Y)
 
             beside(s)
             return carry
 
-        lax.fori_loop(0, slabs, one, 0)
-        for d in range(1, across):
-            piece_copy(slabs - 1, d).wait_recv()
-        for side in range(2):
-            last_send[side] = total(slabs - 1, half if side == 0 else 1 - half).astype(BF16)
-            last_copy(side).start()
-        reduce_y(slabs - 2)
-        for s in range(slabs - 1):
+        lax.fori_loop(0, final, one, 0)
+        for q, here in enumerate(quarters):
+            last_quarter(q).wait_recv()
+            weigh_turned(final, here)
+            both = dot_nn(weighted_t[:, here], flat[here, :])
+            both = both if q == 0 else sums_t[...] + both
+            if q < QUARTERS - 1:
+                sums_t[...] = both
+            else:
+                pieces(final, both)
+            if q == QUARTERS - 2:
+                for s in range(final - LAG_X, final):
+                    reduce_x(s)
+                for s in range(final - LAG_Y, passed):
+                    reduce_y(s)
+        for d in range(slabs):
+            home_copy(d).start()
+        for s in range(passed):
             back_copy(s).wait_recv()
-        for side in range(2):
-            last_copy(side).wait_recv()
+        for i in range(DIRECT):
+            for side in range(2):
+                last_copy(i, side).wait_recv()
+        for d in range(slabs):
+            home_copy(d).wait_recv()
         per = WIDTH // rows
         at_lane = lax.broadcasted_iota(jnp.int32, (rows, WIDTH), 1)
 
         def summed(chunk, part):
             here = slice(part * WIDTH, (part + 1) * WIDTH)
-            if chunk < slabs - 1:
+            if chunk < passed:
                 return back_land[chunk, :, here].astype(F32)
-            return last_land[0, :, here].astype(F32) + last_land[1, :, here].astype(F32)
+            if chunk < final:
+                both = [last_land[chunk - passed, side, :, here] for side in range(2)]
+            else:
+                both = [home_land[d, :, here] for d in range(slabs)]
+            return sum(piece.astype(F32) for piece in both)
 
         for mode in range(MODES):
             for part in range(2):
@@ -565,15 +656,22 @@
                         value + nonlocal_sum[:, lane : lane + WIDTH]
                     )
         for s in range(slabs):
-            if s < slabs - 1:
+            if s < passed:
                 back_copy(s).wait_send()
                 half_copy(s).wait_send()
-            else:
-                last_copy(0).wait_send()
-                last_copy(1).wait_send()
-            for d in range(1, across):
-                piece_copy(s, d).wait_send()
-
+            elif s < final:
+                last_copy(s - passed, 0).wait_send()
+                last_copy(s - passed, 1).wait_send()
+            for d in range(slabs):
+                if s == final:
+                    home_copy(d).wait_send()
+                elif 0 < d < across:
+                    piece_copy(s, d).wait_send()
+
+    for q in range(QUARTERS):
+        last_quarter(q).wait_send()
+    for i in range(2):
+        pl.semaphore_wait(paces.at[i], AHEAD - 1 + SLACK)
     for d in range(1, across):
         proj_x_copy(d).wait_send()
         gather_x(d, x).wait_send()
@@ -644,17 +742,24 @@
             pltpu.VMEM((slabs, rows, part_wide), BF16),
             pltpu.VMEM((slabs, rows, part_wide), BF16),
             pltpu.VMEM((slabs, rows, part_wide), BF16),
-            pltpu.VMEM((2, rows, part_wide), BF16),
-            pltpu.VMEM((2, rows, part_wide), BF16),
-            dma((2, slabs)),
+            pltpu.VMEM((DIRECT, 2, rows, part_wide), BF16),
+            pltpu.VMEM((DIRECT, 2, rows, part_wide), BF16),
+            pltpu.VMEM((slabs, rows, part_wide), BF16),
+            pltpu.VMEM((2 * rows, wide), F32),
+            pltpu.VMEM((part_wide, 2 * bands), F32),
+            dma((2, slabs - 1 + QUARTERS)),
             dma((2, across)),
             dma((2, across)),
-            dma((12,)),
+            dma((8,)),
             dma((2, slabs)),
             dma((2, slabs, across)),
             dma((2, slabs)),
             dma((2, slabs)),
-            dma((8,)),
+            dma((2, DIRECT, 2)),
+            dma((2, slabs)),
+            dma((6,)),
+            dma((2, QUARTERS)),
+            pltpu.SemaphoreType.REGULAR((2,)),
         ],
         compiler_params=pltpu.CompilerParams(
             collective_id=0, has_side_effects=True, vmem_limit_bytes=58 << 20

time: 79.3 us -> 77.8 us (0.981)
  the two profiles are of different devices: /device:TPU:16 before, /device:TPU:6 now
where the time goes in v3:
time: 77.8 us; the launch traced here: 77.6 us
  Pallas kernels  76 us (98%)
  local copies, waits for them, and re-layouts  1.67 us (2%)
    pallas_call x1, Pallas kernels, body(): pl.pallas_call(functools.partial(kernel, (pools, slabs, points, bands)),...  76 us
    unnamed x1, local copies, waits for them, and re-layouts  1.67 us

profile of v3, /device:TPU:6, one launch (start us, length us, event | category | flops | bytes accessed | tf_op | source)
XLA Modules:
  0.0 77.6 jit_solution(12270614891242238670)
XLA Ops:
  0.0 76.0 %matrix_elements.1 = f32[32,4,2,256]{3,2,1,0:T(2,128)} custom-call(bf16[2048,2,256]{2,1,0:T(2,128)(2,1)} %bitcast.5, bf16[4,2,2048]{2,1,0:T(2,128)(2,1)} %pot_in.1, bf16[256,2048]{1,0:T(8,128)(2,1)} %bitcast.6, f32[24,8]{1,0:T(8,128)} %bitcast.8, f32[64,64]{1,0:T(8,128)} %base_in.1, f32[4,2,64,64]{3,2,1,0:T(8,128)} %change_in.1, s32[1,64]{1,0:T(1,128)} %bitcast.9), custom_call_target="tpu_custom_call" | custom-call | tf_op jit(solution)/shard_map/matrix_elements/pallas_call | solution.py:704
  76.0 1.7 %copy.9 = f32[1,32,4,2,256]{4,3,2,1,0:T(2,128)} copy(f32[1,32,4,2,256]{4,3,2,1,0:T(2,128)} %bitcast.7) | data formatting | bytes 524288

commit v4 on v3

--- a/solution.py
+++ b/solution.py
@@ -613,13 +613,12 @@
                 sums_t[...] = both
             else:
                 pieces(final, both)
-            if q == QUARTERS - 2:
-                for s in range(final - LAG_X, final):
-                    reduce_x(s)
-                for s in range(final - LAG_Y, passed):
-                    reduce_y(s)
-        for d in range(slabs):
+        for d in list(range(1, slabs, 2)) + list(range(0, slabs, 2)):
             home_copy(d).start()
+        for s in range(final - LAG_X, final):
+            reduce_x(s)
+        for s in range(final - LAG_Y, passed):
+            reduce_y(s)
         for s in range(passed):
             back_copy(s).wait_recv()
         for i in range(DIRECT):

time: 77.8 us -> 77 us (0.990)
  the two profiles are of different devices: /device:TPU:6 before, /device:TPU:64 now
where the time goes in v4:
time: 77 us; the launch traced here: 76.9 us
  Pallas kernels  75.2 us (98%)
  local copies, waits for them, and re-layouts  1.67 us (2%)
    pallas_call x1, Pallas kernels, body(): pl.pallas_call(functools.partial(kernel, (pools, slabs, points, bands)),...  75.2 us
    unnamed x1, local copies, waits for them, and re-layouts  1.67 us

profile of v4, /device:TPU:64, one launch (start us, length us, event | category | flops | bytes accessed | tf_op | source)
XLA Modules:
  0.0 76.9 jit_solution(13239150715427153313)
XLA Ops:
  0.0 75.2 %matrix_elements.1 = f32[32,4,2,256]{3,2,1,0:T(2,128)} custom-call(bf16[2048,2,256]{2,1,0:T(2,128)(2,1)} %bitcast.5, bf16[4,2,2048]{2,1,0:T(2,128)(2,1)} %pot_in.1, bf16[256,2048]{1,0:T(8,128)(2,1)} %bitcast.6, f32[24,8]{1,0:T(8,128)} %bitcast.8, f32[64,64]{1,0:T(8,128)} %base_in.1, f32[4,2,64,64]{3,2,1,0:T(8,128)} %change_in.1, s32[1,64]{1,0:T(1,128)} %bitcast.9), custom_call_target="tpu_custom_call" | custom-call | tf_op jit(solution)/shard_map/matrix_elements/pallas_call | solution.py:703
  75.2 1.7 %copy.9 = f32[1,32,4,2,256]{4,3,2,1,0:T(2,128)} copy(f32[1,32,4,2,256]{4,3,2,1,0:T(2,128)} %bitcast.7) | data formatting | bytes 524288
